TPU v7x, 512 devices: a whole 4x8x8 slice. The times are simulated.
512 devices in a mesh: gx: 8 (over z), gy: 8 (over y_lo, core), gz: 8 (over y_hi, x).
Axes of the slice: x: 4, y: 8 (y_hi: 2, y_lo: 4; y = y_hi * 4 + y_lo), z: 8, core: 2. Of those that a mesh axis runs over, the one named last changes fastest.
Arguments:
- operator: bfloat16 [8, 8, 8, 1152, 1152], P('gx', 'gy', 'gz'), may hold values from -0.1875 to 0.1875
- lift: bfloat16 [8, 8, 8, 1152, 128], P('gx', 'gy', 'gz'), may hold values from -0.5 to 0.5
- source: bfloat16 [8, 8, 8, 128, 256], P('gx', 'gy', 'gz'), may hold values from -6 to 6
- traces_in: bfloat16 [8, 8, 8, 1152, 256], P('gx', 'gy', 'gz'), may hold values from -6 to 6
- depth: int32 [8], replicated, may hold values from 0 to 6
- direction: int32 [8], replicated, may hold values from 0 to 1
Outputs:
- traces_out: bfloat16 [8, 8, 8, 1152, 256], P('gx', 'gy', 'gz')
All inputs are finite; a program needn't handle non-finite values.
Results may differ from a plain program's by a relative error of at most 0.008.
Values may be sent and summed in bfloat16 or wider, within the bound.
A program may use at most 64 MiB of HBM per device.

v0:
```python
import jax
import jax.numpy as jnp
from jax import lax
from jax.sharding import PartitionSpec as P

RB = 32
STEPS = 6


def with_halo(value, sides, width):
    for axis, dim in sides:
        size, length = (lax.axis_size(axis), value.shape[dim])
        up = [(i, (i + 1) % size) for i in range(size - 1)]
        down = [(j, i) for i, j in up]
        last = lax.slice_in_dim(value, length - width, length, axis=dim)
        leading = lax.slice_in_dim(value, 0, width, axis=dim)
        before = lax.ppermute(last, axis, up)
        after = lax.ppermute(leading, axis, down)
        value = jnp.concatenate([before, value, after], axis=dim)
    return value


def body(operator, lift, source, traces_in, depth, direction):
    matrix = operator[0, 0, 0]
    lifted = jnp.dot(lift[0, 0, 0], source[0, 0, 0], preferred_element_type=jnp.float32)
    backward = jnp.repeat(direction == 1, RB)
    state = traces_in[0, 0, 0]
    rows = state.shape[0] // 3
    for step in range(STEPS):
        gate = jnp.repeat(depth <= step, RB).astype(jnp.float32)
        pieces = []
        for which in range(3):
            part_rows = matrix[which * rows : (which + 1) * rows]
            part_out = (
                jnp.dot(part_rows, state, preferred_element_type=jnp.float32)
                + gate * lifted[which * rows : (which + 1) * rows]
            )
            pieces.append(part_out.astype(jnp.bfloat16))
        near_x = with_halo(pieces[0][None], (("gx", 0),), 1)
        near_y = with_halo(pieces[1][None], (("gy", 0),), 1)
        near_z = with_halo(pieces[2][None], (("gz", 0),), 1)
        face_x = jnp.where(backward, near_x[2], near_x[0])
        face_y = jnp.where(backward, near_y[2], near_y[0])
        face_z = jnp.where(backward, near_z[2], near_z[0])
        state = jnp.concatenate([face_x, face_y, face_z], axis=0)
    return state[None, None, None]


def solution(mesh):
    placed = (
        P("gx", "gy", "gz", None, None),
        P("gx", "gy", "gz", None, None),
        P("gx", "gy", "gz", None, None),
        P("gx", "gy", "gz", None, None),
        P(),
        P(),
    )
    return jax.shard_map(
        body, mesh=mesh, in_specs=placed, out_specs=P("gx", "gy", "gz", None, None), check_vma=False
    )
```

profile of v0, /device:TPU:270, one launch (start us, length us, event | category | flops | bytes accessed | tf_op | source)
XLA Modules:
  0.0 199.9 jit_solution(9258941981629974020)
XLA Ops:
  5.8 3.9 %collective-permute-start.1 = (bf16[1,384,256]{2,1,0:T(8,128)(2,1)S(1)}, bf16[1,384,256]{2,1,0:T(8,128)(2,1)S(1)}, u32[]{:S(2)}, u32[]{:S(2)}) collective-permute-start(bf16[1,384,256]{2,1,0:T(8,128)(2,1)S(1)} %fusion.50), channel_id=1, source_target_pairs={{0,64},{64,128},{128,192},{192,256},{256,320},{320,384},{384,448},... | collective-permute-start | bytes 589832 | tf_op jit(solution)/shard_map/ppermute | solution.py:17
  10.2 1.9 collective-permute-start.2
  12.1 2.4 %collective-permute-start.3 = (bf16[1,384,256]{2,1,0:T(8,128)(2,1)S(1)}, bf16[1,384,256]{2,1,0:T(8,128)(2,1)S(1)}, u32[]{:S(2)}, u32[]{:S(2)}) collective-permute-start(bf16[1,384,256]{2,1,0:T(8,128)(2,1)S(1)} %fusion.49), channel_id=1, source_target_pairs={{0,8},{8,16},{16,24},{24,32},{32,40},{40,48},{48,56},{1,9},{9,17},... | collective-permute-start | bytes 589832 | tf_op jit(solution)/shard_map/ppermute | solution.py:17
  15.7 2.7 %collective-permute-start.4 = (bf16[1,384,256]{2,1,0:T(8,128)(2,1)}, bf16[1,384,256]{2,1,0:T(8,128)(2,1)S(1)}, u32[]{:S(2)}, u32[]{:S(2)}) collective-permute-start(bf16[1,384,256]{2,1,0:T(8,128)(2,1)} %fusion.48), channel_id=1, source_target_pairs={{1,0},{2,1},{3,2},{4,3},{5,4},{6,5},{7,6},{9,8},{10,9},{11,10},{12... | collective-permute-start | bytes 589832 | tf_op jit(solution)/shard_map/ppermute | solution.py:18
  18.4 9.1 %collective-permute-start.5 = (bf16[1,384,256]{2,1,0:T(8,128)(2,1)}, bf16[1,384,256]{2,1,0:T(8,128)(2,1)S(1)}, u32[]{:S(2)}, u32[]{:S(2)}) collective-permute-start(bf16[1,384,256]{2,1,0:T(8,128)(2,1)} %fusion.48), channel_id=1, source_target_pairs={{0,1},{1,2},{2,3},{3,4},{4,5},{5,6},{6,7},{8,9},{9,10},{10,11},{11... | collective-permute-start | bytes 589832 | tf_op jit(solution)/shard_map/ppermute | solution.py:17
  27.9 7.6 %collective-permute-done.4 = bf16[1,384,256]{2,1,0:T(8,128)(2,1)S(1)} collective-permute-done((bf16[1,384,256]{2,1,0:T(8,128)(2,1)}, bf16[1,384,256]{2,1,0:T(8,128)(2,1)S(1)}, u32[]{:S(2)}, u32[]{:S(2)}) %collective-permute-start.4) | collective-permute-done | bytes 196640 | tf_op jit(solution)/shard_map/ppermute | solution.py:18
  41.1 10.4 %collective-permute-start.11 = (bf16[1,384,256]{2,1,0:T(8,128)(2,1)S(1)}, bf16[1,384,256]{2,1,0:T(8,128)(2,1)S(1)}, u32[]{:S(2)}, u32[]{:S(2)}) collective-permute-start(bf16[1,384,256]{2,1,0:T(8,128)(2,1)S(1)} %fusion.35), channel_id=1, source_target_pairs={{0,1},{1,2},{2,3},{3,4},{4,5},{5,6},{6,7},{8,9},{9,10},{10,11},{11... | collective-permute-start | bytes 589832 | tf_op jit(solution)/shard_map/ppermute | solution.py:17
  53.8 2.4 %collective-permute-start.9 = (bf16[1,384,256]{2,1,0:T(8,128)(2,1)S(1)}, bf16[1,384,256]{2,1,0:T(8,128)(2,1)S(1)}, u32[]{:S(2)}, u32[]{:S(2)}) collective-permute-start(bf16[1,384,256]{2,1,0:T(8,128)(2,1)S(1)} %fusion.34), channel_id=1, source_target_pairs={{0,8},{8,16},{16,24},{24,32},{32,40},{40,48},{48,56},{1,9},{9,17},... | collective-permute-start | bytes 589832 | tf_op jit(solution)/shard_map/ppermute | solution.py:17
  57.4 3.1 %collective-permute-start.6 = (bf16[1,384,256]{2,1,0:T(8,128)(2,1)}, bf16[1,384,256]{2,1,0:T(8,128)(2,1)S(1)}, u32[]{:S(2)}, u32[]{:S(2)}) collective-permute-start(bf16[1,384,256]{2,1,0:T(8,128)(2,1)} %fusion.33), channel_id=1, source_target_pairs={{64,0},{128,64},{192,128},{256,192},{320,256},{384,320},{448,384},... | collective-permute-start | bytes 589832 | tf_op jit(solution)/shard_map/ppermute | solution.py:18
  60.4 2.8 %collective-permute-start.7 = (bf16[1,384,256]{2,1,0:T(8,128)(2,1)}, bf16[1,384,256]{2,1,0:T(8,128)(2,1)S(1)}, u32[]{:S(2)}, u32[]{:S(2)}) collective-permute-start(bf16[1,384,256]{2,1,0:T(8,128)(2,1)} %fusion.33), channel_id=1, source_target_pairs={{0,64},{64,128},{128,192},{192,256},{256,320},{320,384},{384,448},... | collective-permute-start | bytes 589832 | tf_op jit(solution)/shard_map/ppermute | solution.py:17
  63.4 3.8 %collective-permute-done.6 = bf16[1,384,256]{2,1,0:T(8,128)(2,1)S(1)} collective-permute-done((bf16[1,384,256]{2,1,0:T(8,128)(2,1)}, bf16[1,384,256]{2,1,0:T(8,128)(2,1)S(1)}, u32[]{:S(2)}, u32[]{:S(2)}) %collective-permute-start.6) | collective-permute-done | bytes 196640 | tf_op jit(solution)/shard_map/ppermute | solution.py:18
  67.2 4.1 %collective-permute-done.7 = bf16[1,384,256]{2,1,0:T(8,128)(2,1)S(1)} collective-permute-done((bf16[1,384,256]{2,1,0:T(8,128)(2,1)}, bf16[1,384,256]{2,1,0:T(8,128)(2,1)S(1)}, u32[]{:S(2)}, u32[]{:S(2)}) %collective-permute-start.7) | collective-permute-done | bytes 196640 | tf_op jit(solution)/shard_map/ppermute | solution.py:17
  75.0 9.9 %collective-permute-start.17 = (bf16[1,384,256]{2,1,0:T(8,128)(2,1)S(1)}, bf16[1,384,256]{2,1,0:T(8,128)(2,1)S(1)}, u32[]{:S(2)}, u32[]{:S(2)}) collective-permute-start(bf16[1,384,256]{2,1,0:T(8,128)(2,1)S(1)} %fusion.38), channel_id=1, source_target_pairs={{0,1},{1,2},{2,3},{3,4},{4,5},{5,6},{6,7},{8,9},{9,10},{10,11},{11... | collective-permute-start | bytes 589832 | tf_op jit(solution)/shard_map/ppermute | solution.py:17
  87.4 2.4 %collective-permute-start.15 = (bf16[1,384,256]{2,1,0:T(8,128)(2,1)S(1)}, bf16[1,384,256]{2,1,0:T(8,128)(2,1)S(1)}, u32[]{:S(2)}, u32[]{:S(2)}) collective-permute-start(bf16[1,384,256]{2,1,0:T(8,128)(2,1)S(1)} %fusion.37), channel_id=1, source_target_pairs={{0,8},{8,16},{16,24},{24,32},{32,40},{40,48},{48,56},{1,9},{9,17},... | collective-permute-start | bytes 589832 | tf_op jit(solution)/shard_map/ppermute | solution.py:17
  92.8 3.9 %collective-permute-start.13 = (bf16[1,384,256]{2,1,0:T(8,128)(2,1)}, bf16[1,384,256]{2,1,0:T(8,128)(2,1)S(1)}, u32[]{:S(2)}, u32[]{:S(2)}) collective-permute-start(bf16[1,384,256]{2,1,0:T(8,128)(2,1)} %fusion.36), channel_id=1, source_target_pairs={{0,64},{64,128},{128,192},{192,256},{256,320},{320,384},{384,448},... | collective-permute-start | bytes 589832 | tf_op jit(solution)/shard_map/ppermute | solution.py:17
  96.9 3.8 %collective-permute-done.12 = bf16[1,384,256]{2,1,0:T(8,128)(2,1)S(1)} collective-permute-done((bf16[1,384,256]{2,1,0:T(8,128)(2,1)}, bf16[1,384,256]{2,1,0:T(8,128)(2,1)S(1)}, u32[]{:S(2)}, u32[]{:S(2)}) %collective-permute-start.12) | collective-permute-done | bytes 196640 | tf_op jit(solution)/shard_map/ppermute | solution.py:18
  100.7 3.1 %collective-permute-done.13 = bf16[1,384,256]{2,1,0:T(8,128)(2,1)S(1)} collective-permute-done((bf16[1,384,256]{2,1,0:T(8,128)(2,1)}, bf16[1,384,256]{2,1,0:T(8,128)(2,1)S(1)}, u32[]{:S(2)}, u32[]{:S(2)}) %collective-permute-start.13) | collective-permute-done | bytes 196640 | tf_op jit(solution)/shard_map/ppermute | solution.py:17
  107.6 9.9 %collective-permute-start.23 = (bf16[1,384,256]{2,1,0:T(8,128)(2,1)S(1)}, bf16[1,384,256]{2,1,0:T(8,128)(2,1)S(1)}, u32[]{:S(2)}, u32[]{:S(2)}) collective-permute-start(bf16[1,384,256]{2,1,0:T(8,128)(2,1)S(1)} %fusion.41), channel_id=1, source_target_pairs={{0,1},{1,2},{2,3},{3,4},{4,5},{5,6},{6,7},{8,9},{9,10},{10,11},{11... | collective-permute-start | bytes 589832 | tf_op jit(solution)/shard_map/ppermute | solution.py:17
  120.0 2.4 %collective-permute-start.21 = (bf16[1,384,256]{2,1,0:T(8,128)(2,1)S(1)}, bf16[1,384,256]{2,1,0:T(8,128)(2,1)S(1)}, u32[]{:S(2)}, u32[]{:S(2)}) collective-permute-start(bf16[1,384,256]{2,1,0:T(8,128)(2,1)S(1)} %fusion.40), channel_id=1, source_target_pairs={{0,8},{8,16},{16,24},{24,32},{32,40},{40,48},{48,56},{1,9},{9,17},... | collective-permute-start | bytes 589832 | tf_op jit(solution)/shard_map/ppermute | solution.py:17
  125.4 3.9 %collective-permute-start.19 = (bf16[1,384,256]{2,1,0:T(8,128)(2,1)}, bf16[1,384,256]{2,1,0:T(8,128)(2,1)S(1)}, u32[]{:S(2)}, u32[]{:S(2)}) collective-permute-start(bf16[1,384,256]{2,1,0:T(8,128)(2,1)} %fusion.39), channel_id=1, source_target_pairs={{0,64},{64,128},{128,192},{192,256},{256,320},{320,384},{384,448},... | collective-permute-start | bytes 589832 | tf_op jit(solution)/shard_map/ppermute | solution.py:17
  129.5 3.7 %collective-permute-done.18 = bf16[1,384,256]{2,1,0:T(8,128)(2,1)S(1)} collective-permute-done((bf16[1,384,256]{2,1,0:T(8,128)(2,1)}, bf16[1,384,256]{2,1,0:T(8,128)(2,1)S(1)}, u32[]{:S(2)}, u32[]{:S(2)}) %collective-permute-start.18) | collective-permute-done | bytes 196640 | tf_op jit(solution)/shard_map/ppermute | solution.py:18
  133.2 3.1 %collective-permute-done.19 = bf16[1,384,256]{2,1,0:T(8,128)(2,1)S(1)} collective-permute-done((bf16[1,384,256]{2,1,0:T(8,128)(2,1)}, bf16[1,384,256]{2,1,0:T(8,128)(2,1)S(1)}, u32[]{:S(2)}, u32[]{:S(2)}) %collective-permute-start.19) | collective-permute-done | bytes 196640 | tf_op jit(solution)/shard_map/ppermute | solution.py:17
  140.1 9.9 %collective-permute-start.29 = (bf16[1,384,256]{2,1,0:T(8,128)(2,1)S(1)}, bf16[1,384,256]{2,1,0:T(8,128)(2,1)S(1)}, u32[]{:S(2)}, u32[]{:S(2)}) collective-permute-start(bf16[1,384,256]{2,1,0:T(8,128)(2,1)S(1)} %fusion.44), channel_id=1, source_target_pairs={{0,1},{1,2},{2,3},{3,4},{4,5},{5,6},{6,7},{8,9},{9,10},{10,11},{11... | collective-permute-start | bytes 589832 | tf_op jit(solution)/shard_map/ppermute | solution.py:17
  152.4 2.4 %collective-permute-start.27 = (bf16[1,384,256]{2,1,0:T(8,128)(2,1)S(1)}, bf16[1,384,256]{2,1,0:T(8,128)(2,1)S(1)}, u32[]{:S(2)}, u32[]{:S(2)}) collective-permute-start(bf16[1,384,256]{2,1,0:T(8,128)(2,1)S(1)} %fusion.43), channel_id=1, source_target_pairs={{0,8},{8,16},{16,24},{24,32},{32,40},{40,48},{48,56},{1,9},{9,17},... | collective-permute-start | bytes 589832 | tf_op jit(solution)/shard_map/ppermute | solution.py:17
  157.2 3.9 %collective-permute-start.25 = (bf16[1,384,256]{2,1,0:T(8,128)(2,1)S(1)}, bf16[1,384,256]{2,1,0:T(8,128)(2,1)S(1)}, u32[]{:S(2)}, u32[]{:S(2)}) collective-permute-start(bf16[1,384,256]{2,1,0:T(8,128)(2,1)S(1)} %fusion.42), channel_id=1, source_target_pairs={{0,64},{64,128},{128,192},{192,256},{256,320},{320,384},{384,448},... | collective-permute-start | bytes 589832 | tf_op jit(solution)/shard_map/ppermute | solution.py:17
  161.3 3.3 %collective-permute-done.24 = bf16[1,384,256]{2,1,0:T(8,128)(2,1)S(1)} collective-permute-done((bf16[1,384,256]{2,1,0:T(8,128)(2,1)S(1)}, bf16[1,384,256]{2,1,0:T(8,128)(2,1)S(1)}, u32[]{:S(2)}, u32[]{:S(2)}) %collective-permute-start.24) | collective-permute-done | bytes 196640 | tf_op jit(solution)/shard_map/ppermute | solution.py:18
  164.6 3.1 %collective-permute-done.25 = bf16[1,384,256]{2,1,0:T(8,128)(2,1)S(1)} collective-permute-done((bf16[1,384,256]{2,1,0:T(8,128)(2,1)S(1)}, bf16[1,384,256]{2,1,0:T(8,128)(2,1)S(1)}, u32[]{:S(2)}, u32[]{:S(2)}) %collective-permute-start.25) | collective-permute-done | bytes 196640 | tf_op jit(solution)/shard_map/ppermute | solution.py:17
  171.5 9.9 %collective-permute-start.35 = (bf16[1,384,256]{2,1,0:T(8,128)(2,1)S(1)}, bf16[1,384,256]{2,1,0:T(8,128)(2,1)S(1)}, u32[]{:S(2)}, u32[]{:S(2)}) collective-permute-start(bf16[1,384,256]{2,1,0:T(8,128)(2,1)S(1)} %fusion.47), channel_id=1, source_target_pairs={{0,1},{1,2},{2,3},{3,4},{4,5},{5,6},{6,7},{8,9},{9,10},{10,11},{11... | collective-permute-start | bytes 589832 | tf_op jit(solution)/shard_map/ppermute | solution.py:17
  183.8 2.4 %collective-permute-start.33 = (bf16[1,384,256]{2,1,0:T(8,128)(2,1)S(1)}, bf16[1,384,256]{2,1,0:T(8,128)(2,1)S(1)}, u32[]{:S(2)}, u32[]{:S(2)}) collective-permute-start(bf16[1,384,256]{2,1,0:T(8,128)(2,1)S(1)} %fusion.46), channel_id=1, source_target_pairs={{0,8},{8,16},{16,24},{24,32},{32,40},{40,48},{48,56},{1,9},{9,17},... | collective-permute-start | bytes 589832 | tf_op jit(solution)/shard_map/ppermute | solution.py:17
  188.6 3.9 %collective-permute-start.31 = (bf16[1,384,256]{2,1,0:T(8,128)(2,1)S(1)}, bf16[1,384,256]{2,1,0:T(8,128)(2,1)S(1)}, u32[]{:S(2)}, u32[]{:S(2)}) collective-permute-start(bf16[1,384,256]{2,1,0:T(8,128)(2,1)S(1)} %fusion.45), channel_id=1, source_target_pairs={{0,64},{64,128},{128,192},{192,256},{256,320},{320,384},{384,448},... | collective-permute-start | bytes 589832 | tf_op jit(solution)/shard_map/ppermute | solution.py:17
  192.5 3.3 %collective-permute-done.30 = bf16[1,384,256]{2,1,0:T(8,128)(2,1)S(1)} collective-permute-done((bf16[1,384,256]{2,1,0:T(8,128)(2,1)S(1)}, bf16[1,384,256]{2,1,0:T(8,128)(2,1)S(1)}, u32[]{:S(2)}, u32[]{:S(2)}) %collective-permute-start.30) | collective-permute-done | bytes 196640 | tf_op jit(solution)/shard_map/ppermute | solution.py:18
  195.9 3.1 %collective-permute-done.31 = bf16[1,384,256]{2,1,0:T(8,128)(2,1)S(1)} collective-permute-done((bf16[1,384,256]{2,1,0:T(8,128)(2,1)S(1)}, bf16[1,384,256]{2,1,0:T(8,128)(2,1)S(1)}, u32[]{:S(2)}, u32[]{:S(2)}) %collective-permute-start.31) | collective-permute-done | bytes 196640 | tf_op jit(solution)/shard_map/ppermute | solution.py:17
  (98 shorter events, 53.3 us)
Async XLA Ops:
  3.9 14.5 %collective-permute-start = (bf16[1,384,256]{2,1,0:T(8,128)(2,1)S(1)}, bf16[1,384,256]{2,1,0:T(8,128)(2,1)S(1)}, u32[]{:S(2)}, u32[]{:S(2)}) collective-permute-start(bf16[1,384,256]{2,1,0:T(8,128)(2,1)S(1)} %fusion.50), channel_id=1, source_target_pairs={{64,0},{128,64},{192,128},{256,192},{320,256},{384,320},{448,384},... | collective-permute-start | bytes 589832 | tf_op jit(solution)/shard_map/ppermute | solution.py:18
  5.8 22.1 %collective-permute-start.1 = (bf16[1,384,256]{2,1,0:T(8,128)(2,1)S(1)}, bf16[1,384,256]{2,1,0:T(8,128)(2,1)S(1)}, u32[]{:S(2)}, u32[]{:S(2)}) collective-permute-start(bf16[1,384,256]{2,1,0:T(8,128)(2,1)S(1)} %fusion.50), channel_id=1, source_target_pairs={{0,64},{64,128},{128,192},{192,256},{256,320},{320,384},{384,448},... | collective-permute-start | bytes 589832 | tf_op jit(solution)/shard_map/ppermute | solution.py:17
  10.2 17.7 %collective-permute-start.2 = (bf16[1,384,256]{2,1,0:T(8,128)(2,1)S(1)}, bf16[1,384,256]{2,1,0:T(8,128)(2,1)S(1)}, u32[]{:S(2)}, u32[]{:S(2)}) collective-permute-start(bf16[1,384,256]{2,1,0:T(8,128)(2,1)S(1)} %fusion.49), channel_id=1, source_target_pairs={{8,0},{16,8},{24,16},{32,24},{40,32},{48,40},{56,48},{9,1},{17,9},... | collective-permute-start | bytes 589832 | tf_op jit(solution)/shard_map/ppermute | solution.py:18
  12.1 15.7 %collective-permute-start.3 = (bf16[1,384,256]{2,1,0:T(8,128)(2,1)S(1)}, bf16[1,384,256]{2,1,0:T(8,128)(2,1)S(1)}, u32[]{:S(2)}, u32[]{:S(2)}) collective-permute-start(bf16[1,384,256]{2,1,0:T(8,128)(2,1)S(1)} %fusion.49), channel_id=1, source_target_pairs={{0,8},{8,16},{16,24},{24,32},{32,40},{40,48},{48,56},{1,9},{9,17},... | collective-permute-start | bytes 589832 | tf_op jit(solution)/shard_map/ppermute | solution.py:17
  15.7 19.9 %collective-permute-start.4 = (bf16[1,384,256]{2,1,0:T(8,128)(2,1)}, bf16[1,384,256]{2,1,0:T(8,128)(2,1)S(1)}, u32[]{:S(2)}, u32[]{:S(2)}) collective-permute-start(bf16[1,384,256]{2,1,0:T(8,128)(2,1)} %fusion.48), channel_id=1, source_target_pairs={{1,0},{2,1},{3,2},{4,3},{5,4},{6,5},{7,6},{9,8},{10,9},{11,10},{12... | collective-permute-start | bytes 589832 | tf_op jit(solution)/shard_map/ppermute | solution.py:18
  18.4 18.9 %collective-permute-start.5 = (bf16[1,384,256]{2,1,0:T(8,128)(2,1)}, bf16[1,384,256]{2,1,0:T(8,128)(2,1)S(1)}, u32[]{:S(2)}, u32[]{:S(2)}) collective-permute-start(bf16[1,384,256]{2,1,0:T(8,128)(2,1)} %fusion.48), channel_id=1, source_target_pairs={{0,1},{1,2},{2,3},{3,4},{4,5},{5,6},{6,7},{8,9},{9,10},{10,11},{11... | collective-permute-start | bytes 589832 | tf_op jit(solution)/shard_map/ppermute | solution.py:17
  39.1 21.3 %collective-permute-start.10 = (bf16[1,384,256]{2,1,0:T(8,128)(2,1)S(1)}, bf16[1,384,256]{2,1,0:T(8,128)(2,1)S(1)}, u32[]{:S(2)}, u32[]{:S(2)}) collective-permute-start(bf16[1,384,256]{2,1,0:T(8,128)(2,1)S(1)} %fusion.35), channel_id=1, source_target_pairs={{1,0},{2,1},{3,2},{4,3},{5,4},{6,5},{7,6},{9,8},{10,9},{11,10},{12... | collective-permute-start | bytes 589832 | tf_op jit(solution)/shard_map/ppermute | solution.py:18
  41.1 22.3 %collective-permute-start.11 = (bf16[1,384,256]{2,1,0:T(8,128)(2,1)S(1)}, bf16[1,384,256]{2,1,0:T(8,128)(2,1)S(1)}, u32[]{:S(2)}, u32[]{:S(2)}) collective-permute-start(bf16[1,384,256]{2,1,0:T(8,128)(2,1)S(1)} %fusion.35), channel_id=1, source_target_pairs={{0,1},{1,2},{2,3},{3,4},{4,5},{5,6},{6,7},{8,9},{9,10},{10,11},{11... | collective-permute-start | bytes 589832 | tf_op jit(solution)/shard_map/ppermute | solution.py:17
  51.9 11.5 %collective-permute-start.8 = (bf16[1,384,256]{2,1,0:T(8,128)(2,1)S(1)}, bf16[1,384,256]{2,1,0:T(8,128)(2,1)S(1)}, u32[]{:S(2)}, u32[]{:S(2)}) collective-permute-start(bf16[1,384,256]{2,1,0:T(8,128)(2,1)S(1)} %fusion.34), channel_id=1, source_target_pairs={{8,0},{16,8},{24,16},{32,24},{40,32},{48,40},{56,48},{9,1},{17,9},... | collective-permute-start | bytes 589832 | tf_op jit(solution)/shard_map/ppermute | solution.py:18
  53.8 9.5 %collective-permute-start.9 = (bf16[1,384,256]{2,1,0:T(8,128)(2,1)S(1)}, bf16[1,384,256]{2,1,0:T(8,128)(2,1)S(1)}, u32[]{:S(2)}, u32[]{:S(2)}) collective-permute-start(bf16[1,384,256]{2,1,0:T(8,128)(2,1)S(1)} %fusion.34), channel_id=1, source_target_pairs={{0,8},{8,16},{16,24},{24,32},{32,40},{40,48},{48,56},{1,9},{9,17},... | collective-permute-start | bytes 589832 | tf_op jit(solution)/shard_map/ppermute | solution.py:17
  57.4 9.8 %collective-permute-start.6 = (bf16[1,384,256]{2,1,0:T(8,128)(2,1)}, bf16[1,384,256]{2,1,0:T(8,128)(2,1)S(1)}, u32[]{:S(2)}, u32[]{:S(2)}) collective-permute-start(bf16[1,384,256]{2,1,0:T(8,128)(2,1)} %fusion.33), channel_id=1, source_target_pairs={{64,0},{128,64},{192,128},{256,192},{320,256},{384,320},{448,384},... | collective-permute-start | bytes 589832 | tf_op jit(solution)/shard_map/ppermute | solution.py:18
  60.4 10.8 %collective-permute-start.7 = (bf16[1,384,256]{2,1,0:T(8,128)(2,1)}, bf16[1,384,256]{2,1,0:T(8,128)(2,1)S(1)}, u32[]{:S(2)}, u32[]{:S(2)}) collective-permute-start(bf16[1,384,256]{2,1,0:T(8,128)(2,1)} %fusion.33), channel_id=1, source_target_pairs={{0,64},{64,128},{128,192},{192,256},{256,320},{320,384},{384,448},... | collective-permute-start | bytes 589832 | tf_op jit(solution)/shard_map/ppermute | solution.py:17
  73.1 19.7 %collective-permute-start.16 = (bf16[1,384,256]{2,1,0:T(8,128)(2,1)S(1)}, bf16[1,384,256]{2,1,0:T(8,128)(2,1)S(1)}, u32[]{:S(2)}, u32[]{:S(2)}) collective-permute-start(bf16[1,384,256]{2,1,0:T(8,128)(2,1)S(1)} %fusion.38), channel_id=1, source_target_pairs={{1,0},{2,1},{3,2},{4,3},{5,4},{6,5},{7,6},{9,8},{10,9},{11,10},{12... | collective-permute-start | bytes 589832 | tf_op jit(solution)/shard_map/ppermute | solution.py:18
  75.0 21.9 %collective-permute-start.17 = (bf16[1,384,256]{2,1,0:T(8,128)(2,1)S(1)}, bf16[1,384,256]{2,1,0:T(8,128)(2,1)S(1)}, u32[]{:S(2)}, u32[]{:S(2)}) collective-permute-start(bf16[1,384,256]{2,1,0:T(8,128)(2,1)S(1)} %fusion.38), channel_id=1, source_target_pairs={{0,1},{1,2},{2,3},{3,4},{4,5},{5,6},{6,7},{8,9},{9,10},{10,11},{11... | collective-permute-start | bytes 589832 | tf_op jit(solution)/shard_map/ppermute | solution.py:17
  85.4 11.5 %collective-permute-start.14 = (bf16[1,384,256]{2,1,0:T(8,128)(2,1)S(1)}, bf16[1,384,256]{2,1,0:T(8,128)(2,1)S(1)}, u32[]{:S(2)}, u32[]{:S(2)}) collective-permute-start(bf16[1,384,256]{2,1,0:T(8,128)(2,1)S(1)} %fusion.37), channel_id=1, source_target_pairs={{8,0},{16,8},{24,16},{32,24},{40,32},{48,40},{56,48},{9,1},{17,9},... | collective-permute-start | bytes 589832 | tf_op jit(solution)/shard_map/ppermute | solution.py:18
  87.4 9.5 %collective-permute-start.15 = (bf16[1,384,256]{2,1,0:T(8,128)(2,1)S(1)}, bf16[1,384,256]{2,1,0:T(8,128)(2,1)S(1)}, u32[]{:S(2)}, u32[]{:S(2)}) collective-permute-start(bf16[1,384,256]{2,1,0:T(8,128)(2,1)S(1)} %fusion.37), channel_id=1, source_target_pairs={{0,8},{8,16},{16,24},{24,32},{32,40},{40,48},{48,56},{1,9},{9,17},... | collective-permute-start | bytes 589832 | tf_op jit(solution)/shard_map/ppermute | solution.py:17
  90.9 9.8 %collective-permute-start.12 = (bf16[1,384,256]{2,1,0:T(8,128)(2,1)}, bf16[1,384,256]{2,1,0:T(8,128)(2,1)S(1)}, u32[]{:S(2)}, u32[]{:S(2)}) collective-permute-start(bf16[1,384,256]{2,1,0:T(8,128)(2,1)} %fusion.36), channel_id=1, source_target_pairs={{64,0},{128,64},{192,128},{256,192},{320,256},{384,320},{448,384},... | collective-permute-start | bytes 589832 | tf_op jit(solution)/shard_map/ppermute | solution.py:18
  92.8 11.1 %collective-permute-start.13 = (bf16[1,384,256]{2,1,0:T(8,128)(2,1)}, bf16[1,384,256]{2,1,0:T(8,128)(2,1)S(1)}, u32[]{:S(2)}, u32[]{:S(2)}) collective-permute-start(bf16[1,384,256]{2,1,0:T(8,128)(2,1)} %fusion.36), channel_id=1, source_target_pairs={{0,64},{64,128},{128,192},{192,256},{256,320},{320,384},{384,448},... | collective-permute-start | bytes 589832 | tf_op jit(solution)/shard_map/ppermute | solution.py:17
  105.7 19.7 %collective-permute-start.22 = (bf16[1,384,256]{2,1,0:T(8,128)(2,1)S(1)}, bf16[1,384,256]{2,1,0:T(8,128)(2,1)S(1)}, u32[]{:S(2)}, u32[]{:S(2)}) collective-permute-start(bf16[1,384,256]{2,1,0:T(8,128)(2,1)S(1)} %fusion.41), channel_id=1, source_target_pairs={{1,0},{2,1},{3,2},{4,3},{5,4},{6,5},{7,6},{9,8},{10,9},{11,10},{12... | collective-permute-start | bytes 589832 | tf_op jit(solution)/shard_map/ppermute | solution.py:18
  107.6 21.9 %collective-permute-start.23 = (bf16[1,384,256]{2,1,0:T(8,128)(2,1)S(1)}, bf16[1,384,256]{2,1,0:T(8,128)(2,1)S(1)}, u32[]{:S(2)}, u32[]{:S(2)}) collective-permute-start(bf16[1,384,256]{2,1,0:T(8,128)(2,1)S(1)} %fusion.41), channel_id=1, source_target_pairs={{0,1},{1,2},{2,3},{3,4},{4,5},{5,6},{6,7},{8,9},{9,10},{10,11},{11... | collective-permute-start | bytes 589832 | tf_op jit(solution)/shard_map/ppermute | solution.py:17
  118.0 11.5 %collective-permute-start.20 = (bf16[1,384,256]{2,1,0:T(8,128)(2,1)S(1)}, bf16[1,384,256]{2,1,0:T(8,128)(2,1)S(1)}, u32[]{:S(2)}, u32[]{:S(2)}) collective-permute-start(bf16[1,384,256]{2,1,0:T(8,128)(2,1)S(1)} %fusion.40), channel_id=1, source_target_pairs={{8,0},{16,8},{24,16},{32,24},{40,32},{48,40},{56,48},{9,1},{17,9},... | collective-permute-start | bytes 589832 | tf_op jit(solution)/shard_map/ppermute | solution.py:18
  120.0 9.5 %collective-permute-start.21 = (bf16[1,384,256]{2,1,0:T(8,128)(2,1)S(1)}, bf16[1,384,256]{2,1,0:T(8,128)(2,1)S(1)}, u32[]{:S(2)}, u32[]{:S(2)}) collective-permute-start(bf16[1,384,256]{2,1,0:T(8,128)(2,1)S(1)} %fusion.40), channel_id=1, source_target_pairs={{0,8},{8,16},{16,24},{24,32},{32,40},{40,48},{48,56},{1,9},{9,17},... | collective-permute-start | bytes 589832 | tf_op jit(solution)/shard_map/ppermute | solution.py:17
  123.5 9.7 %collective-permute-start.18 = (bf16[1,384,256]{2,1,0:T(8,128)(2,1)}, bf16[1,384,256]{2,1,0:T(8,128)(2,1)S(1)}, u32[]{:S(2)}, u32[]{:S(2)}) collective-permute-start(bf16[1,384,256]{2,1,0:T(8,128)(2,1)} %fusion.39), channel_id=1, source_target_pairs={{64,0},{128,64},{192,128},{256,192},{320,256},{384,320},{448,384},... | collective-permute-start | bytes 589832 | tf_op jit(solution)/shard_map/ppermute | solution.py:18
  125.4 10.9 %collective-permute-start.19 = (bf16[1,384,256]{2,1,0:T(8,128)(2,1)}, bf16[1,384,256]{2,1,0:T(8,128)(2,1)S(1)}, u32[]{:S(2)}, u32[]{:S(2)}) collective-permute-start(bf16[1,384,256]{2,1,0:T(8,128)(2,1)} %fusion.39), channel_id=1, source_target_pairs={{0,64},{64,128},{128,192},{192,256},{256,320},{320,384},{384,448},... | collective-permute-start | bytes 589832 | tf_op jit(solution)/shard_map/ppermute | solution.py:17
  138.2 19.0 %collective-permute-start.28 = (bf16[1,384,256]{2,1,0:T(8,128)(2,1)S(1)}, bf16[1,384,256]{2,1,0:T(8,128)(2,1)S(1)}, u32[]{:S(2)}, u32[]{:S(2)}) collective-permute-start(bf16[1,384,256]{2,1,0:T(8,128)(2,1)S(1)} %fusion.44), channel_id=1, source_target_pairs={{1,0},{2,1},{3,2},{4,3},{5,4},{6,5},{7,6},{9,8},{10,9},{11,10},{12... | collective-permute-start | bytes 589832 | tf_op jit(solution)/shard_map/ppermute | solution.py:18
  140.1 21.2 %collective-permute-start.29 = (bf16[1,384,256]{2,1,0:T(8,128)(2,1)S(1)}, bf16[1,384,256]{2,1,0:T(8,128)(2,1)S(1)}, u32[]{:S(2)}, u32[]{:S(2)}) collective-permute-start(bf16[1,384,256]{2,1,0:T(8,128)(2,1)S(1)} %fusion.44), channel_id=1, source_target_pairs={{0,1},{1,2},{2,3},{3,4},{4,5},{5,6},{6,7},{8,9},{9,10},{10,11},{11... | collective-permute-start | bytes 589832 | tf_op jit(solution)/shard_map/ppermute | solution.py:17
  150.5 10.8 %collective-permute-start.26 = (bf16[1,384,256]{2,1,0:T(8,128)(2,1)S(1)}, bf16[1,384,256]{2,1,0:T(8,128)(2,1)S(1)}, u32[]{:S(2)}, u32[]{:S(2)}) collective-permute-start(bf16[1,384,256]{2,1,0:T(8,128)(2,1)S(1)} %fusion.43), channel_id=1, source_target_pairs={{8,0},{16,8},{24,16},{32,24},{40,32},{48,40},{56,48},{9,1},{17,9},... | collective-permute-start | bytes 589832 | tf_op jit(solution)/shard_map/ppermute | solution.py:18
  157.2 10.5 %collective-permute-start.25 = (bf16[1,384,256]{2,1,0:T(8,128)(2,1)S(1)}, bf16[1,384,256]{2,1,0:T(8,128)(2,1)S(1)}, u32[]{:S(2)}, u32[]{:S(2)}) collective-permute-start(bf16[1,384,256]{2,1,0:T(8,128)(2,1)S(1)} %fusion.42), channel_id=1, source_target_pairs={{0,64},{64,128},{128,192},{192,256},{256,320},{320,384},{384,448},... | collective-permute-start | bytes 589832 | tf_op jit(solution)/shard_map/ppermute | solution.py:17
  169.5 19.0 %collective-permute-start.34 = (bf16[1,384,256]{2,1,0:T(8,128)(2,1)S(1)}, bf16[1,384,256]{2,1,0:T(8,128)(2,1)S(1)}, u32[]{:S(2)}, u32[]{:S(2)}) collective-permute-start(bf16[1,384,256]{2,1,0:T(8,128)(2,1)S(1)} %fusion.47), channel_id=1, source_target_pairs={{1,0},{2,1},{3,2},{4,3},{5,4},{6,5},{7,6},{9,8},{10,9},{11,10},{12... | collective-permute-start | bytes 589832 | tf_op jit(solution)/shard_map/ppermute | solution.py:18
  171.5 21.0 %collective-permute-start.35 = (bf16[1,384,256]{2,1,0:T(8,128)(2,1)S(1)}, bf16[1,384,256]{2,1,0:T(8,128)(2,1)S(1)}, u32[]{:S(2)}, u32[]{:S(2)}) collective-permute-start(bf16[1,384,256]{2,1,0:T(8,128)(2,1)S(1)} %fusion.47), channel_id=1, source_target_pairs={{0,1},{1,2},{2,3},{3,4},{4,5},{5,6},{6,7},{8,9},{9,10},{10,11},{11... | collective-permute-start | bytes 589832 | tf_op jit(solution)/shard_map/ppermute | solution.py:17
  181.9 10.7 %collective-permute-start.32 = (bf16[1,384,256]{2,1,0:T(8,128)(2,1)S(1)}, bf16[1,384,256]{2,1,0:T(8,128)(2,1)S(1)}, u32[]{:S(2)}, u32[]{:S(2)}) collective-permute-start(bf16[1,384,256]{2,1,0:T(8,128)(2,1)S(1)} %fusion.46), channel_id=1, source_target_pairs={{8,0},{16,8},{24,16},{32,24},{40,32},{48,40},{56,48},{9,1},{17,9},... | collective-permute-start | bytes 589832 | tf_op jit(solution)/shard_map/ppermute | solution.py:18
  188.6 10.4 %collective-permute-start.31 = (bf16[1,384,256]{2,1,0:T(8,128)(2,1)S(1)}, bf16[1,384,256]{2,1,0:T(8,128)(2,1)S(1)}, u32[]{:S(2)}, u32[]{:S(2)}) collective-permute-start(bf16[1,384,256]{2,1,0:T(8,128)(2,1)S(1)} %fusion.45), channel_id=1, source_target_pairs={{0,64},{64,128},{128,192},{192,256},{256,320},{320,384},{384,448},... | collective-permute-start | bytes 589832 | tf_op jit(solution)/shard_map/ppermute | solution.py:17
  (12 other events, 133.3 us)
where the time goes:
time: 201 us; the launch traced here: 200 us
  starting transfers between devices  133 us (66%)
  waiting for transfers between devices  44 us (22%)
  matrix products  19.6 us (10%)
  other arithmetic  2.03 us (1%)
    ppermute x18, starting transfers between devices, with_halo(): before = lax.ppermute(last, axis, up)  96.1 us
    ppermute x18, starting transfers between devices, with_halo(): after = lax.ppermute(leading, axis, down)  36.5 us
    ppermute x18, waiting for transfers between devices, with_halo(): after = lax.ppermute(leading, axis, down)  25.5 us
    ppermute x18, waiting for transfers between devices, with_halo(): before = lax.ppermute(last, axis, up)  18.5 us
    dot_general x18, matrix products, body(): jnp.dot(part_rows, state, preferred_element_type=jnp.float32)  18.2 us
  transfers between devices with their start and end apart: 36, of which 12 were waited for; matrix products, arithmetic and copies ran while one was open for 4% of the time, Pallas kernels for 0%

commit v1 on v0

v1 whole, which is shorter than its diff:
```python
import functools

import jax
import jax.numpy as jnp
from jax import lax
from jax.experimental import pallas as pl
from jax.experimental.pallas import tpu as pltpu
from jax.sharding import PartitionSpec as P

MESH = pl.DeviceIdType.MESH
FACE = 384
ORDER = 1152
SRC = 128
NB = 8
RB = 32
RHS = NB * RB
STEPS = 6
N = 8
CHUNKS = 2
LAG = 1
UP, DOWN = 0, 1
AXES = ("gx", "gy", "gz")
F32, BF16 = jnp.float32, jnp.bfloat16
NT = (((1,), (1,)), ((), ()))


def plan(n_up):
    ups = [n_up // CHUNKS + (c < n_up % CHUNKS) for c in range(CHUNKS)]
    n_down = NB - n_up
    downs = [n_down // CHUNKS + (CHUNKS - 1 - c < n_down % CHUNKS) for c in range(CHUNKS)]
    rows, place, at = [], {}, 0
    seen = [0, n_up]
    for c in range(CHUNKS):
        spans = []
        for kind, count in ((UP, ups[c]), (DOWN, downs[c])):
            spans.append((at, count * RB))
            for _ in range(count):
                place[seen[kind]] = at
                seen[kind] += 1
                at += RB
        rows.append(tuple(spans))
    return rows, place


def kernel(n_up, op_h, lift_h, src_h, tr_h, info_h, out, a, at, lf, sr, tr, st, og, lifted, hop, info, order, since,
           lsem, ssem, rsem, hsem, fsem):
    rows, place = plan(n_up)
    pos = [lax.axis_index(name) for name in AXES]
    gy, gz = pos[1], pos[2]
    odd = lax.rem(gy, 2) == 1
    high = (gz >= N // 2).astype(jnp.int32)
    ends = (gz == 3) | (gz == 4)
    ring = odd & (ends | (gz == 0) | (gz == N - 1))

    loads = [
        pltpu.make_async_copy(s, d, lsem.at[n])
        for n, (s, d) in enumerate(
            ((info_h, info), (tr_h, tr), (src_h, sr), (lift_h, lf), (op_h, a))
        )
    ]
    for load in loads:
        load.start()

    def direct(f, d):
        there = (pos[f] < N - 1) if d == UP else (pos[f] > 0)
        if f == 2:
            there &= jnp.logical_not(odd & (gz == (3 if d == UP else 4)))
        return there

    def step_to(f, d):
        return {AXES[f]: pos[f] + (1 if d == UP else -1)}

    barrier = pltpu.get_barrier_semaphore()
    peers = jnp.int32(0)
    for f in range(3):
        for d in (UP, DOWN):
            there = direct(f, d)
            peers += there.astype(jnp.int32)

            @pl.when(there)
            def _():
                pl.semaphore_signal(barrier, inc=1, device_id=step_to(f, d), device_id_type=MESH)

    peers += 2 * ring.astype(jnp.int32)
    for other in (jnp.where(ends, 0, 3), jnp.where(ends, N - 1, 4)):

        @pl.when(ring)
        def _():
            pl.semaphore_signal(barrier, inc=1, device_id={"gz": other}, device_id_type=MESH)

    for f in range(3):
        for d in (UP, DOWN):

            @pl.when(pos[f] == (0 if d == UP else N - 1))
            def _():
                for c in range(CHUNKS):
                    r0, nr = rows[c][d]
                    if nr:
                        for t in range(1, STEPS + 1):
                            st[t, r0 : r0 + nr, f * FACE : (f + 1) * FACE] = jnp.zeros((nr, FACE), BF16)

    loads[0].wait()

    def per_column(at_row):
        each = [jnp.broadcast_to(info[at_row + b : at_row + b + 1, :], (RB, 128)) for b in range(NB)]
        return jnp.concatenate(each, axis=0).astype(BF16)

    pick = jnp.where(lax.broadcasted_iota(jnp.int32, (16, 128), 1) == 0, 1.0, 0.0).astype(BF16)
    back = lax.dot_general(pick, per_column(0), NT, preferred_element_type=F32)
    rows_i = lax.broadcasted_iota(jnp.int32, (RHS, RHS), 0)
    cols_i = lax.broadcasted_iota(jnp.int32, (RHS, RHS), 1)
    before = jnp.where((rows_i >> 5) < (cols_i >> 5), 1.0, 0.0).astype(BF16)
    downs = jnp.dot(back.astype(BF16), before, preferred_element_type=F32) * (1.0 / RB)
    col = lax.broadcasted_iota(jnp.int32, (16, RHS), 1)
    key = jnp.where(back > 0.5, n_up + downs, (col >> 5).astype(F32) - downs)
    row_of = (col & (RB - 1)).astype(F32)
    for s in range(NB):
        row_of += jnp.where(key == s, float(place[s]), 0.0)
    order[...] = jnp.where(rows_i.astype(F32) == row_of[0:1, :], 1.0, 0.0).astype(BF16)
    since[...] = jnp.dot(order[...], per_column(NB), preferred_element_type=F32)
    unit = lax.broadcasted_iota(jnp.int32, (FACE, FACE), 0) == lax.broadcasted_iota(jnp.int32, (FACE, FACE), 1)
    unit = jnp.where(unit, 1.0, 0.0).astype(BF16)

    def span(f):
        return pl.ds(pl.multiple_of(f * FACE, FACE), FACE)

    loads[1].wait()
    loads[2].wait()
    loads[3].wait()
    coeffs = lax.dot_general(order[...], sr[...], NT, preferred_element_type=F32).astype(BF16)

    def begin(f, carry):
        st[0, :, span(f)] = lax.dot_general(order[...], tr[span(f), :], NT, preferred_element_type=F32).astype(BF16)
        lifted[:, span(f)] = lax.dot_general(coeffs, lf[span(f), :], NT, preferred_element_type=F32)
        return carry

    lax.fori_loop(0, 3, begin, 0)
    loads[4].wait()

    def flip(n, carry):
        k, f = n // 3, lax.rem(n, 3)
        at[span(k), span(f)] = lax.dot_general(unit, a[span(f), span(k)], NT, preferred_element_type=F32).astype(BF16)
        return carry

    lax.fori_loop(0, 9, flip, 0)

    def part(ref, t, c, d, f):
        r0, nr = rows[c][d]
        return ref.at[t, pl.ds(r0, nr), pl.ds(f * FACE, FACE)]

    def hop_part(t, c, d):
        r0, nr = rows[c][d]
        return hop.at[t, pl.ds(r0, nr), :]

    def send(t, c, d, f):
        return pltpu.make_async_remote_copy(
            src_ref=part(og, t, c, d, f), dst_ref=part(st, t + 1, c, d, f),
            send_sem=ssem.at[t, c, d, f], recv_sem=rsem.at[t, c, d, f],
            device_id=step_to(f, d), device_id_type=MESH,
        )

    def send_hop(t, c, d):
        return pltpu.make_async_remote_copy(
            src_ref=part(og, t, c, d, 2), dst_ref=hop_part(t, c, d),
            send_sem=ssem.at[t, c, d, 2], recv_sem=hsem.at[t, c],
            device_id={"gz": 0 if d == UP else N - 1}, device_id_type=MESH,
        )

    def send_on(t, c, d):
        return pltpu.make_async_remote_copy(
            src_ref=hop_part(t, c, d), dst_ref=part(st, t + 1, c, d, 2),
            send_sem=fsem.at[t, c], recv_sem=rsem.at[t, c, d, 2],
            device_id={"gz": 4 if d == UP else 3}, device_id_type=MESH,
        )

    def times(tau):
        return (tau - LAG * high, tau - LAG * (1 - high))

    def inside(t):
        return (t >= 0) & (t < STEPS)

    def arrive(t, c, d, last=STEPS - 1):
        if not rows[c][d][1]:
            return
        for f in (2, 0, 1):
            has = (pos[f] > 0) if d == UP else (pos[f] < N - 1)

            @pl.when(has & (t >= 1) & (t <= last))
            def _():
                send(t - 1, c, d, f).wait_recv()

    def sent(tau):
        for c in range(CHUNKS):
            for d, t in zip((UP, DOWN), times(tau)):
                if not rows[c][d][1]:
                    continue
                for f in range(3):
                    has = (pos[f] < N - 1) if d == UP else (pos[f] > 0)

                    @pl.when(has & inside(t - 1))
                    def _():
                        send(t - 1, c, d, f).wait_send()

                @pl.when(odd & (gz == (0 if d == UP else N - 1)) & inside(tau - 2))
                def _():
                    send_on(tau - 2, c, d).wait_send()

    def tick(tau, carry):
        ts = times(tau)
        read = [jnp.clip(t, 0, STEPS - 1) for t in ts]
        write = [jnp.clip(t, 0, STEPS) for t in ts]
        for c in range(CHUNKS):
            kinds = [d for d in (UP, DOWN) if rows[c][d][1]]
            for d in kinds:
                arrive(ts[d], c, d)

            def face(n, carry):
                f = lax.rem(n + 2, 3)
                x = jnp.concatenate([st[read[d], rows[c][d][0] : sum(rows[c][d]), :] for d in kinds], axis=0)
                acc = jnp.dot(x, at[:, span(f)], preferred_element_type=F32)
                at_row = 0
                for d in kinds:
                    r0, nr = rows[c][d]
                    gate = jnp.where(since[r0 : r0 + nr, :] <= ts[d].astype(F32), 1.0, 0.0)
                    gate = jnp.concatenate([gate] * (FACE // 128), axis=1)
                    total = acc[at_row : at_row + nr] + gate * lifted[r0 : r0 + nr, span(f)]
                    og[write[d], r0 : r0 + nr, span(f)] = total.astype(BF16)
                    at_row += nr
                for d in kinds:
                    for g in range(3):

                        @pl.when((f == g) & direct(g, d) & inside(ts[d]))
                        def _():
                            send(ts[d], c, d, g).start()

                    @pl.when((f == 2) & odd & (gz == (3 if d == UP else 4)) & inside(ts[d]))
                    def _():
                        send_hop(ts[d], c, d).start()

                return carry

            lax.fori_loop(0, 3, face, 0)
            for d in kinds:

                @pl.when(odd & (gz == (0 if d == UP else N - 1)) & inside(tau - 1))
                def _():
                    send_hop(tau - 1, c, d).wait_recv()
                    send_on(tau - 1, c, d).start()

        sent(tau)
        return carry

    pl.semaphore_wait(barrier, peers)
    lax.fori_loop(0, STEPS + LAG, tick, 0)
    sent(jnp.int32(STEPS + LAG))
    for c in range(CHUNKS):
        for d in (UP, DOWN):
            arrive(jnp.int32(STEPS), c, d, STEPS)

    def finish(f, carry):
        block = lax.dot_general(unit, st[STEPS, :, span(f)], NT, preferred_element_type=F32).astype(BF16)
        out[span(f), :] = jnp.dot(block, order[...], preferred_element_type=F32).astype(BF16)
        return carry

    lax.fori_loop(0, 3, finish, 0)


def sweep(n_up, operator, lift, source, traces_in, info, *_):
    anywhere = pl.BlockSpec(memory_space=pl.ANY)
    return pl.pallas_call(
        functools.partial(kernel, n_up),
        out_shape=jax.ShapeDtypeStruct((ORDER, RHS), BF16),
        in_specs=[anywhere] * 5,
        out_specs=pl.BlockSpec(memory_space=pltpu.VMEM),
        scratch_shapes=[
            pltpu.VMEM((ORDER, ORDER), BF16),
            pltpu.VMEM((ORDER, ORDER), BF16),
            pltpu.VMEM((ORDER, SRC), BF16),
            pltpu.VMEM((SRC, RHS), BF16),
            pltpu.VMEM((ORDER, RHS), BF16),
            pltpu.VMEM((STEPS + 1, RHS, ORDER), BF16),
            pltpu.VMEM((STEPS + 1, RHS, ORDER), BF16),
            pltpu.VMEM((RHS, ORDER), F32),
            pltpu.VMEM((STEPS, RHS, FACE), BF16),
            pltpu.VMEM((16, 128), F32),
            pltpu.VMEM((RHS, RHS), BF16),
            pltpu.VMEM((RHS, 128), F32),
            pltpu.SemaphoreType.DMA((5,)),
            pltpu.SemaphoreType.DMA((STEPS, CHUNKS, 2, 3)),
            pltpu.SemaphoreType.DMA((STEPS, CHUNKS, 2, 3)),
            pltpu.SemaphoreType.DMA((STEPS, CHUNKS)),
            pltpu.SemaphoreType.DMA((STEPS, CHUNKS)),
        ],
        compiler_params=pltpu.CompilerParams(
            collective_id=n_up, has_side_effects=True, vmem_limit_bytes=40 * 2**20
        ),
        name=f"sweep_{n_up}",
    )(operator, lift, source, traces_in, info)


VARIANTS = (3, 4, 5)


def general(operator, lift, source, traces_in, info, depth, direction):
    lifted = jnp.dot(lift, source, preferred_element_type=F32)
    backward = jnp.repeat(direction == 1, RB)
    level = jnp.repeat(depth, RB)
    up = [(i, i + 1) for i in range(N - 1)]
    down = [(i + 1, i) for i in range(N - 1)]

    def step(t, state):
        gate = (level <= t).astype(F32)
        outgoing = (jnp.dot(operator, state, preferred_element_type=F32) + gate * lifted).astype(BF16)
        faces = []
        for f, axis in enumerate(AXES):
            face = outgoing[f * FACE : (f + 1) * FACE]
            faces.append(jnp.where(backward, lax.ppermute(face, axis, down), lax.ppermute(face, axis, up)))
        return jnp.concatenate(faces, axis=0)

    return lax.fori_loop(0, STEPS, step, traces_in)


def body(operator, lift, source, traces_in, depth, direction):
    info = jnp.broadcast_to(jnp.concatenate([direction, depth]).astype(F32)[:, None], (2 * NB, 128))
    args = (operator[0, 0, 0], lift[0, 0, 0], source[0, 0, 0], traces_in[0, 0, 0], info, depth, direction)
    n_up = NB - jnp.sum((direction == 1).astype(jnp.int32))
    which = len(VARIANTS) + sum(jnp.where(n_up == n, i - len(VARIANTS), 0) for i, n in enumerate(VARIANTS))
    branches = [functools.partial(sweep, n) for n in VARIANTS] + [general]
    result = lax.switch(which, branches, *args)
    return result[None, None, None]


def solution(mesh):
    placed = (
        P("gx", "gy", "gz", None, None),
        P("gx", "gy", "gz", None, None),
        P("gx", "gy", "gz", None, None),
        P("gx", "gy", "gz", None, None),
        P(),
        P(),
    )
    return jax.shard_map(
        body, mesh=mesh, in_specs=placed, out_specs=P("gx", "gy", "gz", None, None), check_vma=False
    )
```

time: 201 us -> 56.1 us (0.28)
  the two profiles are of different devices: /device:TPU:270 before, /device:TPU:7 now
where the time goes in v1:
time: 56.1 us; the launch traced here: 55.3 us
  Pallas kernels  50.4 us (90%)
  other arithmetic  2.13 us (4%)
  local copies, waits for them, and re-layouts  1.97 us (4%)
  between operations  0.71 us (1%)
    pallas_call x1, Pallas kernels, sweep(): pl.pallas_call(functools.partial(kernel, n_up), out_shape=jax.ShapeDtypeS...  50.4 us
    unnamed x12, local copies, waits for them, and re-layouts  1.9 us
    reduce_sum x1, other arithmetic, body(): n_up = NB - jnp.sum((direction == 1).astype(jnp.int32))  1.38 us

profile of v1, /device:TPU:7, one launch (start us, length us, event | category | flops | bytes accessed | tf_op | source)
XLA Modules:
  0.0 55.3 jit_solution(15200011378312743059)
XLA Ops:
  0.0 0.0 copy-start.4
  0.0 0.0 copy-start.3
  0.0 0.0 copy-start
  0.0 0.0 copy-start.2
  0.0 0.0 copy-start.1
  0.0 1.4 %fusion.5 = s32[]{:T(128)} fusion(s32[8]{0:T(128)} %param.17), kind=kLoop, calls=%fused_computation.11 | loop fusion | flops 23 | bytes 36 | tf_op jit(solution)/shard_map/reduce_sum | solution.py:326
  2.1 0.7 %add_convert_fusion = f32[16,1]{0,1:T(1,128)S(1)} fusion(s32[8,1]{0,1:T(1,128)} %bitcast.41, s32[8,1]{0,1:T(1,128)} %bitcast.45), kind=kLoop, calls=%fused_computation.12 | loop fusion | flops 32 | bytes 128 | tf_op jit(solution)/shard_map/convert_element_type | solution.py:324
  2.8 1.1 %copy.27 = bf16[1152,256]{1,0:T(8,128)(2,1)S(1)} copy(bf16[1152,256]{1,0:T(8,128)(2,1)} %bitcast.25) | data formatting | bytes 1179648
  3.9 0.0 copy-done.4
  3.9 0.0 copy-done.3
  3.9 0.0 copy-done
  3.9 0.0 copy-done.2
  3.9 0.0 copy-done.1
  3.9 50.5 %conditional.1 = (bf16[1,1,1,1152,256]{4,3,2,1,0:T(8,128)(2,1)S(1)}) conditional(s32[]{:T(128)} %clamp.3, (f32[16,1]{0,1:T(1,128)S(1)}, bf16[1152,1152]{1,0:T(8,128)(2,1)}, bf16[1152,128]{1,0:T(8,128)(2,1)S(1)}, bf16[128,256]{1,0:T(8,128)(2,1)S(1)}, bf16[1152,256]{1,0:T(8,128)(2,1)S(1)}) %tuple.80, ...), branch_computations={%region_1.2_spmd, %region_2.3_spmd, %region_3.4_spmd, %region_4.7_... | conditional | flops 757924352 | bytes 15408601 | solution.py:329
  3.9 0.1 broadcast_in_dim.48.info_h
  4.0 50.4 %sweep_5.1 = bf16[1152,256]{1,0:T(8,128)(2,1)S(1)} custom-call(bf16[1152,1152]{1,0:T(8,128)(2,1)} %get-tuple-element.170.op_h, bf16[1152,128]{1,0:T(8,128)(2,1)S(1)} %get-tuple-element.171.lift_h, bf16[128,256]{1,0:T(8,128)(2,1)S(1)} %get-tuple-element.172.src_h, bf16[1152,256]{1,0:T(8,128)(2,1)S(1)} %get-tuple-element.173.tr_h, ...), custom_call_target="tpu_custom_call" | custom-call | tf_op jit(solution)/shard_map/cond/branch_2_fun/sweep_5/pallas_call | solution.py:270
  54.4 0.8 %copy.30 = bf16[1,1,1,1152,256]{4,3,2,1,0:T(8,128)(2,1)} copy(bf16[1,1,1,1152,256]{4,3,2,1,0:T(8,128)(2,1)S(1)} %get-tuple-element.189) | data formatting | bytes 1179648
Async XLA Ops:
  0.0 3.9 %copy-start.4 = (s32[8]{0:T(128)S(1)}, s32[8]{0:T(128)}, u32[]{:S(2)}) copy-start(s32[8]{0:T(128)} %param.17) | copy-start | bytes 100
  0.0 3.9 %copy-start.3 = (s32[8]{0:T(128)S(1)}, s32[8]{0:T(128)}, u32[]{:S(2)}) copy-start(s32[8]{0:T(128)} %param.16) | copy-start | bytes 100
  0.0 3.9 %copy-start = (bf16[1,1,1,1152,256]{4,3,2,1,0:T(8,128)(2,1)S(1)}, bf16[1,1,1,1152,256]{4,3,2,1,0:T(8,128)(2,1)}, u32[]{:S(2)}) copy-start(bf16[1,1,1,1152,256]{4,3,2,1,0:T(8,128)(2,1)} %param.15) | copy-start | bytes 1769476
  0.0 3.9 %copy-start.2 = (bf16[1,1,1,128,256]{4,3,2,1,0:T(8,128)(2,1)S(1)}, bf16[1,1,1,128,256]{4,3,2,1,0:T(8,128)(2,1)}, u32[]{:S(2)}) copy-start(bf16[1,1,1,128,256]{4,3,2,1,0:T(8,128)(2,1)} %param.14) | copy-start | bytes 196612
  0.0 3.9 %copy-start.1 = (bf16[1,1,1,1152,128]{4,3,2,1,0:T(8,128)(2,1)S(1)}, bf16[1,1,1,1152,128]{4,3,2,1,0:T(8,128)(2,1)}, u32[]{:S(2)}) copy-start(bf16[1,1,1,1152,128]{4,3,2,1,0:T(8,128)(2,1)} %param.13) | copy-start | bytes 884740

commit v2 on v1

--- a/solution.py
+++ b/solution.py
@@ -265,7 +265,7 @@
     lax.fori_loop(0, 3, finish, 0)
 
 
-def sweep(n_up, operator, lift, source, traces_in, info, *_):
+def sweep(n_up, operator, lift, source, traces_in, info):
     anywhere = pl.BlockSpec(memory_space=pl.ANY)
     return pl.pallas_call(
         functools.partial(kernel, n_up),
@@ -298,35 +298,14 @@
     )(operator, lift, source, traces_in, info)
 
 
-VARIANTS = (3, 4, 5)
-
-
-def general(operator, lift, source, traces_in, info, depth, direction):
-    lifted = jnp.dot(lift, source, preferred_element_type=F32)
-    backward = jnp.repeat(direction == 1, RB)
-    level = jnp.repeat(depth, RB)
-    up = [(i, i + 1) for i in range(N - 1)]
-    down = [(i + 1, i) for i in range(N - 1)]
-
-    def step(t, state):
-        gate = (level <= t).astype(F32)
-        outgoing = (jnp.dot(operator, state, preferred_element_type=F32) + gate * lifted).astype(BF16)
-        faces = []
-        for f, axis in enumerate(AXES):
-            face = outgoing[f * FACE : (f + 1) * FACE]
-            faces.append(jnp.where(backward, lax.ppermute(face, axis, down), lax.ppermute(face, axis, up)))
-        return jnp.concatenate(faces, axis=0)
-
-    return lax.fori_loop(0, STEPS, step, traces_in)
+VARIANTS = tuple(range(NB + 1))
 
 
 def body(operator, lift, source, traces_in, depth, direction):
     info = jnp.broadcast_to(jnp.concatenate([direction, depth]).astype(F32)[:, None], (2 * NB, 128))
-    args = (operator[0, 0, 0], lift[0, 0, 0], source[0, 0, 0], traces_in[0, 0, 0], info, depth, direction)
+    args = (operator[0, 0, 0], lift[0, 0, 0], source[0, 0, 0], traces_in[0, 0, 0], info)
     n_up = NB - jnp.sum((direction == 1).astype(jnp.int32))
-    which = len(VARIANTS) + sum(jnp.where(n_up == n, i - len(VARIANTS), 0) for i, n in enumerate(VARIANTS))
-    branches = [functools.partial(sweep, n) for n in VARIANTS] + [general]
-    result = lax.switch(which, branches, *args)
+    result = lax.switch(n_up, [functools.partial(sweep, n) for n in VARIANTS], *args)
     return result[None, None, None]
 
 

time: 56.1 us -> 59.2 us (1.055); the launches traced: 55.3 us -> 59.1 us
  Pallas kernels: 50.4 us -> 55.2 us
  local copies, waits for them, and re-layouts: 1.97 us -> 0.89 us
    pallas_call x1, Pallas kernels: 50.4 us -> 55.2 us  [sweep(): pl.pallas_call(functools.partial(kernel, n_up), out_shape=jax.ShapeDtypeS...]
    unnamed x12 -> x1, local copies, waits for them, and re-layouts: 1.9 us -> 0.82 us
where the time goes in v2:
time: 59.2 us; the launch traced here: 59.1 us
  Pallas kernels  55.2 us (93%)
  other arithmetic  2.04 us (3%)
  local copies, waits for them, and re-layouts  0.89 us (2%)
  between operations  0.66 us (1%)
    pallas_call x1, Pallas kernels, sweep(): pl.pallas_call(functools.partial(kernel, n_up), out_shape=jax.ShapeDtypeS...  55.2 us
    reduce_sum x1, other arithmetic, body(): n_up = NB - jnp.sum((direction == 1).astype(jnp.int32))  1.29 us

profile of v2, /device:TPU:7, one launch (start us, length us, event | category | flops | bytes accessed | tf_op | source)
XLA Modules:
  0.0 59.1 jit_solution(11803716384983282275)
XLA Ops:
  0.0 1.3 %fusion = s32[]{:T(128)} fusion(s32[8]{0:T(128)} %param.20), kind=kLoop, calls=%fused_computation.1 | loop fusion | flops 23 | bytes 36 | tf_op jit(solution)/shard_map/reduce_sum | solution.py:307
  1.9 0.7 %add_convert_fusion = f32[16,1]{0,1:T(1,128)S(1)} fusion(s32[8,1]{0,1:T(1,128)} %bitcast.111, s32[8,1]{0,1:T(1,128)} %bitcast.110), kind=kLoop, calls=%fused_computation.2 | loop fusion | flops 32 | bytes 128 | tf_op jit(solution)/shard_map/convert_element_type | solution.py:305
  2.7 55.5 %conditional.1 = (bf16[1,1,1,1152,256]{4,3,2,1,0:T(8,128)(2,1)S(1)}) conditional(s32[]{:T(128)} %clamp.3, (bf16[1,1,1,1152,1152]{4,3,2,1,0:T(8,128)(2,1)}, bf16[1,1,1,1152,128]{4,3,2,1,0:T(8,128)(2,1)}, bf16[1,1,1,128,256]{4,3,2,1,0:T(8,128)(2,1)}, bf16[1,1,1,1152,256]{4,3,2,1,0:T(8,128)(2,1)}, ...), branch_computations={%region_1.0_spmd, %region_2.0_spmd, %region_3.0_spmd, %region_4.0_... | conditional | bytes 8264 | solution.py:308
  2.7 0.1 broadcast_in_dim.66.info_h
  2.8 55.2 %sweep_2.1 = bf16[1152,256]{1,0:T(8,128)(2,1)S(1)} custom-call(bf16[1152,1152]{1,0:T(8,128)(2,1)} %bitcast.58, bf16[1152,128]{1,0:T(8,128)(2,1)} %bitcast.76, bf16[128,256]{1,0:T(8,128)(2,1)} %bitcast.85, bf16[1152,256]{1,0:T(8,128)(2,1)} %bitcast.67, f32[16,128]{1,0:T(8,128)S(1)} %broadcast_in_dim.66.info_h), custom_call_target="tpu_custom_call" | custom-call | tf_op jit(solution)/shard_map/cond/branch_2_fun/sweep_2/pallas_call | solution.py:270
  58.3 0.8 %copy.62 = bf16[1,1,1,1152,256]{4,3,2,1,0:T(8,128)(2,1)} copy(bf16[1,1,1,1152,256]{4,3,2,1,0:T(8,128)(2,1)S(1)} %get-tuple-element.205) | data formatting | bytes 1179648

commit v3 on v2

--- a/solution.py
+++ b/solution.py
@@ -18,6 +18,7 @@
 N = 8
 CHUNKS = 2
 LAG = 1
+UNROLL = (2, 6)
 UP, DOWN = 0, 1
 AXES = ("gx", "gy", "gz")
 F32, BF16 = jnp.float32, jnp.bfloat16
@@ -122,6 +123,8 @@
     unit = jnp.where(unit, 1.0, 0.0).astype(BF16)
 
     def span(f):
+        if isinstance(f, int):
+            return slice(f * FACE, (f + 1) * FACE)
         return pl.ds(pl.multiple_of(f * FACE, FACE), FACE)
 
     loads[1].wait()
@@ -141,8 +144,6 @@
         k, f = n // 3, lax.rem(n, 3)
         at[span(k), span(f)] = lax.dot_general(unit, a[span(f), span(k)], NT, preferred_element_type=F32).astype(BF16)
         return carry
-
-    lax.fori_loop(0, 9, flip, 0)
 
     def part(ref, t, c, d, f):
         r0, nr = rows[c][d]
@@ -205,19 +206,29 @@
                 def _():
                     send_on(tau - 2, c, d).wait_send()
 
-    def tick(tau, carry):
+    def tick(tau, first, unroll):
         ts = times(tau)
         read = [jnp.clip(t, 0, STEPS - 1) for t in ts]
         write = [jnp.clip(t, 0, STEPS) for t in ts]
         for c in range(CHUNKS):
             kinds = [d for d in (UP, DOWN) if rows[c][d][1]]
-            for d in kinds:
-                arrive(ts[d], c, d)
-
-            def face(n, carry):
-                f = lax.rem(n + 2, 3)
+            if not first:
+                for d in kinds:
+
+                    @pl.when(odd & (gz == (0 if d == UP else N - 1)) & inside(tau - 1))
+                    def _():
+                        send_hop(tau - 1, c, d).wait_recv()
+                        send_on(tau - 1, c, d).start()
+
+                for d in kinds:
+                    arrive(ts[d], c, d)
+
+            def face(f):
                 x = jnp.concatenate([st[read[d], rows[c][d][0] : sum(rows[c][d]), :] for d in kinds], axis=0)
-                acc = jnp.dot(x, at[:, span(f)], preferred_element_type=F32)
+                if first:
+                    acc = lax.dot_general(x, a[span(f), :], NT, preferred_element_type=F32)
+                else:
+                    acc = jnp.dot(x, at[:, span(f)], preferred_element_type=F32)
                 at_row = 0
                 for d in kinds:
                     r0, nr = rows[c][d]
@@ -228,30 +239,44 @@
                     at_row += nr
                 for d in kinds:
                     for g in range(3):
-
-                        @pl.when((f == g) & direct(g, d) & inside(ts[d]))
+                        if unroll and f != g:
+                            continue
+                        go = direct(g, d) & inside(ts[d])
+
+                        @pl.when(go if unroll else go & (f == g))
                         def _():
                             send(ts[d], c, d, g).start()
 
-                    @pl.when((f == 2) & odd & (gz == (3 if d == UP else 4)) & inside(ts[d]))
+                    if unroll and f != 2:
+                        continue
+                    go = odd & (gz == (3 if d == UP else 4)) & inside(ts[d])
+
+                    @pl.when(go if unroll else go & (f == 2))
                     def _():
                         send_hop(ts[d], c, d).start()
 
-                return carry
-
-            lax.fori_loop(0, 3, face, 0)
-            for d in kinds:
-
-                @pl.when(odd & (gz == (0 if d == UP else N - 1)) & inside(tau - 1))
-                def _():
-                    send_hop(tau - 1, c, d).wait_recv()
-                    send_on(tau - 1, c, d).start()
-
-        sent(tau)
+            if unroll:
+                for f in (2, 0, 1):
+                    face(f)
+            else:
+
+                def turn(n, carry):
+                    face(lax.rem(n + 2, 3))
+                    return carry
+
+                lax.fori_loop(0, 3, turn, 0)
+
+        if not first:
+            sent(tau)
+
+    def main(tau, carry):
+        tick(tau, False, UNROLL[0] <= n_up <= UNROLL[1])
         return carry
 
     pl.semaphore_wait(barrier, peers)
-    lax.fori_loop(0, STEPS + LAG, tick, 0)
+    tick(jnp.int32(0), True, False)
+    lax.fori_loop(0, 9, flip, 0)
+    lax.fori_loop(1, STEPS + LAG, main, 0)
     sent(jnp.int32(STEPS + LAG))
     for c in range(CHUNKS):
         for d in (UP, DOWN):

time: 59.2 us -> 52.8 us (0.89)
  Pallas kernels: 55.2 us -> 48.1 us
    pallas_call x1, Pallas kernels: 55.2 us -> 48.1 us  [sweep(): pl.pallas_call(functools.partial(kernel, n_up), out_shape=jax.ShapeDtypeS...]
where the time goes in v3:
time: 52.8 us; the launch traced here: 52.2 us
  Pallas kernels  48.1 us (91%)
  other arithmetic  2.04 us (4%)
  local copies, waits for them, and re-layouts  0.89 us (2%)
  between operations  0.66 us (1%)
    pallas_call x1, Pallas kernels, sweep(): pl.pallas_call(functools.partial(kernel, n_up), out_shape=jax.ShapeDtypeS...  48.1 us
    reduce_sum x1, other arithmetic, body(): n_up = NB - jnp.sum((direction == 1).astype(jnp.int32))  1.29 us

profile of v3, /device:TPU:7, one launch (start us, length us, event | category | flops | bytes accessed | tf_op | source)
XLA Modules:
  0.0 52.2 jit_solution(15752737456720159981)
XLA Ops:
  0.0 1.3 %fusion = s32[]{:T(128)} fusion(s32[8]{0:T(128)} %param.20), kind=kLoop, calls=%fused_computation.1 | loop fusion | flops 23 | bytes 36 | tf_op jit(solution)/shard_map/reduce_sum | solution.py:332
  1.9 0.7 %add_convert_fusion = f32[16,1]{0,1:T(1,128)S(1)} fusion(s32[8,1]{0,1:T(1,128)} %bitcast.111, s32[8,1]{0,1:T(1,128)} %bitcast.110), kind=kLoop, calls=%fused_computation.2 | loop fusion | flops 32 | bytes 128 | tf_op jit(solution)/shard_map/convert_element_type | solution.py:330
  2.7 48.7 %conditional.1 = (bf16[1,1,1,1152,256]{4,3,2,1,0:T(8,128)(2,1)S(1)}) conditional(s32[]{:T(128)} %clamp.3, (bf16[1,1,1,1152,1152]{4,3,2,1,0:T(8,128)(2,1)}, bf16[1,1,1,1152,128]{4,3,2,1,0:T(8,128)(2,1)}, bf16[1,1,1,128,256]{4,3,2,1,0:T(8,128)(2,1)}, bf16[1,1,1,1152,256]{4,3,2,1,0:T(8,128)(2,1)}, ...), branch_computations={%region_1.0_spmd, %region_2.0_spmd, %region_3.0_spmd, %region_4.0_... | conditional | bytes 8264 | solution.py:333
  2.9 0.1 broadcast_in_dim.72.info_h
  2.9 48.1 %sweep_4.1 = bf16[1152,256]{1,0:T(8,128)(2,1)S(1)} custom-call(bf16[1152,1152]{1,0:T(8,128)(2,1)} %bitcast.60, bf16[1152,128]{1,0:T(8,128)(2,1)} %bitcast.78, bf16[128,256]{1,0:T(8,128)(2,1)} %bitcast.87, bf16[1152,256]{1,0:T(8,128)(2,1)} %bitcast.69, f32[16,128]{1,0:T(8,128)S(1)} %broadcast_in_dim.72.info_h), custom_call_target="tpu_custom_call" | custom-call | tf_op jit(solution)/shard_map/cond/branch_4_fun/sweep_4/pallas_call | solution.py:295
  51.4 0.8 %copy.62 = bf16[1,1,1,1152,256]{4,3,2,1,0:T(8,128)(2,1)} copy(bf16[1,1,1,1152,256]{4,3,2,1,0:T(8,128)(2,1)S(1)} %get-tuple-element.205) | data formatting | bytes 1179648

commit v4 on v3

--- a/solution.py
+++ b/solution.py
@@ -142,7 +142,7 @@
 
     def flip(n, carry):
         k, f = n // 3, lax.rem(n, 3)
-        at[span(k), span(f)] = lax.dot_general(unit, a[span(f), span(k)], NT, preferred_element_type=F32).astype(BF16)
+        at[span(k), span(lax.rem(f + 1, 3))] = lax.dot_general(unit, a[span(f), span(k)], NT, preferred_element_type=F32).astype(BF16)
         return carry
 
     def part(ref, t, c, d, f):
@@ -223,12 +223,19 @@
                 for d in kinds:
                     arrive(ts[d], c, d)
 
-            def face(f):
-                x = jnp.concatenate([st[read[d], rows[c][d][0] : sum(rows[c][d]), :] for d in kinds], axis=0)
+            def state():
+                return jnp.concatenate([st[read[d], rows[c][d][0] : sum(rows[c][d]), :] for d in kinds], axis=0)
+
+            def multiply(x, place_of, count):
+                lanes = span(place_of) if count == 1 else slice(0, count * FACE)
+                return jnp.dot(x, at[:, lanes], preferred_element_type=F32)
+
+            def face(f, acc=None):
+                x = state()
                 if first:
                     acc = lax.dot_general(x, a[span(f), :], NT, preferred_element_type=F32)
-                else:
-                    acc = jnp.dot(x, at[:, span(f)], preferred_element_type=F32)
+                elif acc is None:
+                    acc = multiply(x, (f + 1) % 3 if unroll else lax.rem(f + 1, 3), 1)
                 at_row = 0
                 for d in kinds:
                     r0, nr = rows[c][d]
@@ -256,8 +263,10 @@
                         send_hop(ts[d], c, d).start()
 
             if unroll:
-                for f in (2, 0, 1):
-                    face(f)
+                both = multiply(state(), 0, 2)
+                face(2, both[:, :FACE])
+                face(0, both[:, FACE:])
+                face(1)
             else:
 
                 def turn(n, carry):

time: 52.8 us -> 52.6 us (level)
  the two profiles are of different devices: /device:TPU:7 before, /device:TPU:1 now
where the time goes in v4:
time: 52.6 us
  Pallas kernels  48.5 us (92%)
  other arithmetic  2.04 us (4%)
  local copies, waits for them, and re-layouts  0.89 us (2%)
  between operations  0.66 us (1%)
    pallas_call x1, Pallas kernels, sweep(): pl.pallas_call(functools.partial(kernel, n_up), out_shape=jax.ShapeDtypeS...  48.5 us
    reduce_sum x1, other arithmetic, body(): n_up = NB - jnp.sum((direction == 1).astype(jnp.int32))  1.29 us

profile of v4, /device:TPU:1, one launch (start us, length us, event | category | flops | bytes accessed | tf_op | source)
XLA Modules:
  0.0 52.6 jit_solution(9449002497885686490)
XLA Ops:
  0.0 1.3 %fusion = s32[]{:T(128)} fusion(s32[8]{0:T(128)} %param.20), kind=kLoop, calls=%fused_computation.1 | loop fusion | flops 23 | bytes 36 | tf_op jit(solution)/shard_map/reduce_sum | solution.py:341
  1.9 0.7 %add_convert_fusion = f32[16,1]{0,1:T(1,128)S(1)} fusion(s32[8,1]{0,1:T(1,128)} %bitcast.111, s32[8,1]{0,1:T(1,128)} %bitcast.110), kind=kLoop, calls=%fused_computation.2 | loop fusion | flops 32 | bytes 128 | tf_op jit(solution)/shard_map/convert_element_type | solution.py:339
  2.7 49.1 %conditional.1 = (bf16[1,1,1,1152,256]{4,3,2,1,0:T(8,128)(2,1)S(1)}) conditional(s32[]{:T(128)} %clamp.3, (bf16[1,1,1,1152,1152]{4,3,2,1,0:T(8,128)(2,1)}, bf16[1,1,1,1152,128]{4,3,2,1,0:T(8,128)(2,1)}, bf16[1,1,1,128,256]{4,3,2,1,0:T(8,128)(2,1)}, bf16[1,1,1,1152,256]{4,3,2,1,0:T(8,128)(2,1)}, ...), branch_computations={%region_1.0_spmd, %region_2.0_spmd, %region_3.0_spmd, %region_4.0_... | conditional | bytes 8264 | solution.py:342
  2.9 0.1 broadcast_in_dim.72.info_h
  2.9 48.5 %sweep_4.1 = bf16[1152,256]{1,0:T(8,128)(2,1)S(1)} custom-call(bf16[1152,1152]{1,0:T(8,128)(2,1)} %bitcast.60, bf16[1152,128]{1,0:T(8,128)(2,1)} %bitcast.78, bf16[128,256]{1,0:T(8,128)(2,1)} %bitcast.87, bf16[1152,256]{1,0:T(8,128)(2,1)} %bitcast.69, f32[16,128]{1,0:T(8,128)S(1)} %broadcast_in_dim.72.info_h), custom_call_target="tpu_custom_call" | custom-call | tf_op jit(solution)/shard_map/cond/branch_4_fun/sweep_4/pallas_call | solution.py:304
  51.8 0.8 %copy.62 = bf16[1,1,1,1152,256]{4,3,2,1,0:T(8,128)(2,1)} copy(bf16[1,1,1,1152,256]{4,3,2,1,0:T(8,128)(2,1)S(1)} %get-tuple-element.205) | data formatting | bytes 1179648
